TPU v7x, 256 devices: a whole 4x4x8 slice. The times are simulated.
256 devices in a mesh: ctx: 16 (over z_lo, y), fsdp: 16 (over z_hi, x, core).
Axes of the slice: x: 4, y: 4, z: 8 (z_hi: 2, z_lo: 4; z = z_hi * 4 + z_lo), core: 2. Of those that a mesh axis runs over, the one named last changes fastest.
Arguments:
- hidden_in: bfloat16 [16, 1024, 7168], P('fsdp', 'ctx'), may hold values from -4 to 4
- queries: bfloat16 [16, 1024, 18432], P('fsdp', 'ctx'), may hold values from -18 to 18
- span_latent: bfloat16 [16, 1024, 576], P('fsdp', 'ctx'), may hold values from -7 to 7
- cache_latent: bfloat16 [16, 1024, 576], P('fsdp', 'ctx'), may hold values from -4 to 4
- cache_len: int32 [16, 16], P('fsdp'), may hold values from 1 to 64, 512 in all within a row
- value_up: bfloat16 [32, 512, 128], P('ctx'), may hold values from -1 to 1
- out_proj: bfloat16 [7168, 4096], P('fsdp', 'ctx'), may hold values from -0.09375 to 0.09375
- norm_gain: float32 [7168], replicated, may hold values from 0.5 to 2
- expert_gate: bfloat16 [7168, 4096], P('fsdp', 'ctx'), may hold values from -0.0625 to 0.0625
- expert_up: bfloat16 [7168, 4096], P('fsdp', 'ctx'), may hold values from -0.0625 to 0.0625
- expert_down: bfloat16 [7168, 4096], P('fsdp', 'ctx'), may hold values from -0.125 to 0.125
- routes: int32 [16, 1024, 8], P('fsdp'), may hold values from 0 to 383, as said below
- route_weights: float32 [16, 1024, 8], P('fsdp'), may hold values from 0.2 to 1
Outputs:
- layer_out: bfloat16 [16, 1024, 7168], P('fsdp', 'ctx')
Inputs may be any that keep to these rules, and one draw needn't show every extreme that they name: `routes`: each token names 8 different experts. Each expert below 2 is named by at most 4 of the 64 tokens of one span slice, and by exactly 4 in some slice of every sequence.
All inputs are finite; a program needn't handle non-finite values.
Results may differ from a plain program's by a relative error of at most 0.023.
Values may be sent and summed in bfloat16 or wider, within the bound.
A program may use at most 128 MiB of HBM per device.

v0:
```python
import jax
import jax.numpy as jnp
from jax import lax
from jax.sharding import PartitionSpec as P

FF_EXP = 2048
CAP = 4


SOFTMAX_SCALE = 192.0 ** (-0.5)
EPSILON = 1e-06
NEGATIVE = -1e30
FAR_RANK = 1 << 30


def window_slots(routed, weighted, parts, per_part, capacity, flight):
    expert_ids = jnp.arange(flight, dtype=jnp.int32)
    matched = routed[:, :, None] == expert_ids[None, None, :]
    hitting = jnp.any(matched, axis=1).astype(jnp.int32)
    gate_token = jnp.sum(jnp.where(matched, weighted[:, :, None], 0.0), axis=1)
    blocked = hitting.reshape(parts, per_part, flight)
    within = jnp.cumsum(blocked, axis=1) - blocked
    slot_row = (jnp.arange(parts, dtype=jnp.int32)[:, None, None] * capacity + within).reshape(
        parts * per_part, flight
    )
    slot_ids = jnp.arange(parts * capacity, dtype=jnp.int32)
    selector = (slot_row.T[:, None, :] == slot_ids[None, :, None]) & (hitting.T[:, None, :] == 1)
    gate_slot = jnp.sum(jnp.where(selector, gate_token.T[:, None, :], 0.0), axis=2)
    return (selector, gate_slot)


def attend(query_block, query_pos, key_local, lengths, cache_dev, span_dev, latent):
    heads_here = query_block.shape[1]
    rows_here = query_block.shape[0]
    per_device = cache_dev + span_dev
    device_ids = jnp.arange(lengths.shape[0], dtype=jnp.int32)
    running = jnp.full((heads_here, rows_here), NEGATIVE, jnp.float32)
    key_piece = lax.all_gather(key_local, "ctx", axis=1, tiled=True)[0]
    key_count = key_piece.shape[0]
    position = jnp.arange(key_count, dtype=jnp.int32)
    owner_dev = position // per_device
    offset = position - owner_dev * per_device
    length_at = jnp.sum(
        jnp.where(owner_dev[:, None] == device_ids[None, :], lengths[None, :], 0), axis=1
    )
    cached_rank = jnp.where(offset < length_at, -1, FAR_RANK)
    key_rank = jnp.where(offset < cache_dev, cached_rank, owner_dev * span_dev + offset - cache_dev)
    visible = key_rank[None, None, :] <= query_pos[None, :, None]
    scores = (
        jnp.einsum("qhd,kd->hqk", query_block, key_piece, preferred_element_type=jnp.float32)
        * SOFTMAX_SCALE
    )
    scores = jnp.where(visible, scores, NEGATIVE)
    newmax = jnp.maximum(running, jnp.max(scores, axis=2))
    exp_terms = jnp.where(visible, jnp.exp(scores - newmax[:, :, None]), 0.0)
    denominator = jnp.sum(exp_terms, axis=2)
    accumulated = jnp.einsum(
        "hqk,kd->hqd",
        exp_terms.astype(jnp.bfloat16),
        key_piece[:, :latent],
        preferred_element_type=jnp.float32,
    )
    running, denominator, accumulated = (newmax, denominator, accumulated)
    return (accumulated / denominator[:, :, None]).astype(jnp.bfloat16)


def body(
    hidden_in,
    queries,
    span_latent,
    cache_latent,
    cache_len,
    value_up,
    out_proj,
    norm_gain,
    expert_gate,
    expert_up,
    expert_down,
    routes,
    route_weights,
):
    ctx_count = lax.axis_size("ctx")
    ctx_index = lax.axis_index("ctx")
    span_dev = hidden_in.shape[1]
    cache_dev = cache_latent.shape[1]
    width_qk = span_latent.shape[2]
    latent = value_up.shape[1]
    heads_all = queries.shape[2] // width_qk
    hidden_here = expert_gate.shape[1]
    flight = ctx_count * hidden_here // FF_EXP
    span_all = span_dev * ctx_count
    proj_full, gate_full, up_full, down_full = (
        lax.all_gather(out_proj, "fsdp", axis=0, tiled=True),
        lax.all_gather(expert_gate, "fsdp", axis=0, tiled=True),
        lax.all_gather(expert_up, "fsdp", axis=0, tiled=True),
        lax.all_gather(expert_down, "fsdp", axis=0, tiled=True),
    )
    key_local = jnp.concatenate([cache_latent[0], span_latent[0]], axis=0)[None]
    lengths = cache_len[0]
    query_local = queries[0].reshape(span_dev, heads_all, width_qk)
    query_heads = lax.all_to_all(query_local, "ctx", split_axis=1, concat_axis=0, tiled=True)
    attended = attend(
        query_heads,
        jnp.arange(span_all, dtype=jnp.int32),
        key_local,
        lengths,
        cache_dev,
        span_dev,
        latent,
    )
    head_out = jnp.einsum(
        "gtl,glv->tgv", attended, value_up, preferred_element_type=jnp.float32
    ).astype(jnp.bfloat16)
    head_out = head_out.reshape(span_all, -1)
    selector, gate_slot = window_slots(
        routes[0], route_weights[0], ctx_count, span_dev, CAP, flight
    )
    picker = selector.astype(jnp.bfloat16)
    picked = jnp.einsum("esr,rj->esj", picker, head_out, preferred_element_type=jnp.float32).astype(
        jnp.bfloat16
    )
    partial_rows = jnp.einsum("esj,dj->esd", picked, proj_full, preferred_element_type=jnp.float32)
    own_picker = lax.dynamic_slice_in_dim(picker, ctx_index * span_dev, span_dev, 2)
    partial_rows = partial_rows + jnp.einsum(
        "esr,rd->esd", own_picker, hidden_in[0], preferred_element_type=jnp.float32
    )
    mixed_rows = lax.psum(partial_rows.astype(jnp.bfloat16), "ctx").astype(jnp.float32)
    own_expert = ctx_index * hidden_here // FF_EXP
    own_rows = lax.dynamic_index_in_dim(mixed_rows, own_expert, 0, keepdims=False)
    mean_square = jnp.mean(own_rows * own_rows, axis=1, keepdims=True)
    normed = (own_rows * lax.rsqrt(mean_square + EPSILON) * norm_gain).astype(jnp.bfloat16)
    gate_proj = jnp.dot(normed, gate_full, preferred_element_type=jnp.float32)
    up_proj = jnp.dot(normed, up_full, preferred_element_type=jnp.float32)
    activated = (jax.nn.silu(gate_proj) * up_proj).astype(jnp.bfloat16)
    own_gate = lax.dynamic_index_in_dim(gate_slot, own_expert, 0, keepdims=False)
    expert_rows = (
        jnp.einsum("sf,df->sd", activated, down_full, preferred_element_type=jnp.float32)
        * own_gate[:, None]
    )
    picker_wide = lax.dynamic_index_in_dim(selector, own_expert, 0, keepdims=False).astype(
        jnp.float32
    )
    head_term = jnp.einsum("rj,dj->rd", head_out, proj_full, preferred_element_type=jnp.float32)
    summed = lax.psum_scatter(
        (
            head_term
            + jnp.einsum("sr,sd->rd", picker_wide, expert_rows, precision=lax.Precision.HIGHEST)
        ).astype(jnp.bfloat16),
        "ctx",
        scatter_dimension=0,
        tiled=True,
    ).astype(jnp.float32)
    return (hidden_in[0].astype(jnp.float32) + summed).astype(jnp.bfloat16)[None]


def solution(mesh):
    in_specs = (
        P("fsdp", "ctx", None),
        P("fsdp", "ctx", None),
        P("fsdp", "ctx", None),
        P("fsdp", "ctx", None),
        P("fsdp", None),
        P("ctx", None, None),
        P("fsdp", "ctx"),
        P(),
        P("fsdp", "ctx"),
        P("fsdp", "ctx"),
        P("fsdp", "ctx"),
        P("fsdp", None, None),
        P("fsdp", None, None),
    )
    out_specs = P("fsdp", "ctx", None)
    return jax.shard_map(body, mesh=mesh, in_specs=in_specs, out_specs=out_specs, check_vma=False)
```

profile of v0, /device:TPU:10, one launch (start us, length us, event | category | flops | bytes accessed | tf_op | source)
XLA Modules:
  0.0 796.1 jit_solution(3860066107008711057)
XLA Ops:
  9.4 4.5 reshape_squeeze.3
  13.9 2.4 copy.56
  16.4 9.1 %all-to-all-start = ((bf16[64,32,576]{2,0,1:T(8,128)(2,1)}), bf16[64,32,576]{2,0,1:T(8,128)(2,1)S(1)}, u32[]{:S(2)}, u32[]{:S(2)}) async-start(bf16[64,32,576]{2,0,1:T(8,128)(2,1)} %copy.56), calls=%async_computation | async-start | bytes 5242880 | tf_op jit(solution)/shard_map/all_to_all | solution.py:101
  30.2 2.3 iota_compare_fusion
  32.5 55.2 %all-to-all-done = bf16[64,32,576]{2,0,1:T(8,128)(2,1)S(1)} async-done(((bf16[64,32,576]{2,0,1:T(8,128)(2,1)}), bf16[64,32,576]{2,0,1:T(8,128)(2,1)S(1)}, u32[]{:S(2)}, u32[]{:S(2)}) %all-to-all-start) | async-done | bytes 2359328 | tf_op jit(solution)/shard_map/all_to_all | solution.py:101
  87.7 1.8 copy.57
  89.5 27.9 %all-gather.15.cloned.1.call-done = bf16[2048,576]{0,1:T(8,128)(2,1)} async-done(((bf16[128,576]{0,1:T(8,128)(2,1)}), bf16[2048,576]{0,1:T(8,128)(2,1)}) %all-gather.15.cloned.1.call-update) | async-done | bytes 2359312 | tf_op jit(solution)/shard_map/all_gather | solution.py:38
  117.4 11.8 %fusion = (f32[2,1024]{1,0:T(2,128)S(1)}, f32[2048,1024,2]{1,0,2:T(8,128)S(1)}) fusion(pred[1024,2048]{0,1:T(8,128)(4,1)} %iota_compare_fusion, bf16[1024,2,576]{2,0,1:T(8,128)(2,1)} %bitcast.88, bf16[2048,576]{0,1:T(8,128)(2,1)} %all-gather.15.cloned.1.call-done), kind=kOutput, calls=%fused_computation.3 | convolution fusion | flops 4844419072 | bytes 23601152 | tf_op jit(solution)/shard_map/qhd,kd->hqk/dot_general | solution.py:50
  129.2 5.7 copy-done.2
  134.9 4.5 fusion.1
  139.4 11.2 %fusion.15 = bf16[2,1024,128]{1,2,0:T(8,128)(2,1)S(1)} fusion(bf16[2,512,128]{2,1,0:T(8,128)(2,1)S(1)} %copy-done, f32[2,1024]{1,0:T(2,128)S(1)} %fusion.1, f32[2048,1024,2]{1,0,2:T(8,128)} %copy-done.2, f32[2,1024]{1,0:T(2,128)S(1)} %broadcast_maximum_fusion, pred[1024,2048]{0,1:T(8,128)(4,1)S(1)} %copy-done.4, ...), kind=kOutput, calls=%fused_computation.25 | convolution fusion | flops 4586733568 | bytes 21774336 | tf_op jit(solution)/shard_map/gtl,glv->tgv/dot_general | solution.py:111
  150.6 48.4 %all-gather.7.cloned.1.call-done = bf16[7168,256]{1,0:T(8,128)(2,1)} async-done(((bf16[448,256]{1,0:T(8,128)(2,1)}), bf16[7168,256]{1,0:T(8,128)(2,1)}) %all-gather.7.cloned.1.call-update) | async-done | bytes 3670032 | tf_op jit(solution)/shard_map/all_gather | solution.py:93
  199.0 5.7 fusion.7
  204.7 4.0 fusion.3
  210.7 160.1 %all-reduce.2.cloned.1.call-done = bf16[2,64,7168]{2,1,0:T(8,128)(2,1)} async-done(((bf16[2,64,7168]{2,1,0:T(8,128)(2,1)}), bf16[2,64,7168]{2,1,0:T(8,128)(2,1)}) %all-reduce.2.cloned.1.call-update) | async-done | bytes 1835024 | tf_op jit(solution)/shard_map/psum | solution.py:127
  372.3 73.4 %all-gather.9.cloned.1.call-done = bf16[7168,256]{1,0:T(8,128)(2,1)} async-done(((bf16[448,256]{1,0:T(8,128)(2,1)}), bf16[7168,256]{1,0:T(8,128)(2,1)}) %all-gather.9.cloned.1.call-update) | async-done | bytes 3670032 | tf_op jit(solution)/shard_map/all_gather | solution.py:94
  445.7 3.1 fusion.29
  448.8 69.1 %all-gather.11.cloned.1.call-done = bf16[7168,256]{1,0:T(8,128)(2,1)} async-done(((bf16[448,256]{1,0:T(8,128)(2,1)}), bf16[7168,256]{1,0:T(8,128)(2,1)}) %all-gather.11.cloned.1.call-update) | async-done | bytes 3670032 | tf_op jit(solution)/shard_map/all_gather | solution.py:95
  517.9 72.2 %all-gather.13.cloned.1.call-done = bf16[7168,256]{1,0:T(8,128)(2,1)} async-done(((bf16[448,256]{1,0:T(8,128)(2,1)}), bf16[7168,256]{1,0:T(8,128)(2,1)}) %all-gather.13.cloned.1.call-update) | async-done | bytes 3670032 | tf_op jit(solution)/shard_map/all_gather | solution.py:96
  590.2 6.2 convolution_multiply_fusion
  596.4 15.6 %fusion.24 = f32[1024,7168]{1,0:T(8,128)} fusion(f32[64,7168]{1,0:T(8,128)S(1)} %convolution_multiply_fusion, pred[2,64,1024]{2,1,0:T(32,128)(4,1)S(1)} %copy-done.6, s32[]{:T(128)S(6)} %select_n.77), kind=kOutput, calls=%fused_computation.34 | convolution fusion | flops 5637144576 | bytes 31260676 | tf_op jit(solution)/shard_map/sr,sd->rd/dot_general | solution.py:147
  612.0 17.1 %add_convert_fusion = bf16[1024,7168]{1,0:T(8,128)(2,1)} fusion(f32[1024,7168]{1,0:T(8,128)} %fusion.24, bf16[1024,256]{0,1:T(8,128)(2,1)S(1)} %bitcast.90, bf16[7168,256]{1,0:T(8,128)(2,1)S(1)} %copy-done.3), kind=kOutput, calls=%fused_computation | convolution fusion | flops 3772776448 | bytes 48234496 | tf_op jit(solution)/shard_map/rj,dj->rd/dot_general | solution.py:143
  629.1 157.8 %reduce-scatter.2.cloned.1.call-done = bf16[64,7168]{1,0:T(8,128)(2,1)} async-done(((bf16[1024,7168]{1,0:T(8,128)(2,1)}), bf16[64,7168]{1,0:T(8,128)(2,1)}) %reduce-scatter.2.cloned.1.call-update) | async-done | bytes 917520 | tf_op jit(solution)/shard_map/reduce_scatter | solution.py:144
  787.0 2.3 fusion.17
  (61 shorter events, 11.0 us)
Async XLA Ops:
  6.5 132.8 %copy-start = (bf16[2,512,128]{2,1,0:T(8,128)(2,1)S(1)}, bf16[2,512,128]{2,1,0:T(8,128)(2,1)}, u32[]{:S(2)}) copy-start(bf16[2,512,128]{2,1,0:T(8,128)(2,1)} %param.18) | copy-start | bytes 786436
  6.5 110.9 %all-gather.15.cloned.1.call-start = ((), (), s32[]{:S(2)}) async-start(), calls=%async_computation.8 | async-start | bytes 2506752 | tf_op jit(solution)/shard_map/all_gather | solution.py:38
  16.4 10.1 %copy-start.7 = (s32[1,1024,8]{1,2,0:T(8,128)S(1)}, s32[1,1024,8]{1,2,0:T(8,128)}, u32[]{:S(2)}) copy-start(s32[1,1024,8]{1,2,0:T(8,128)} %param.24) | copy-start | bytes 98308
  16.4 12.9 %copy-start.11 = (s32[1,16]{1,0:T(1,128)S(1)}, s32[1,16]{1,0:T(1,128)}, u32[]{:S(2)}) copy-start(s32[1,16]{1,0:T(1,128)} %param.17) | copy-start | bytes 196
  16.4 71.3 %all-to-all-start = ((bf16[64,32,576]{2,0,1:T(8,128)(2,1)}), bf16[64,32,576]{2,0,1:T(8,128)(2,1)S(1)}, u32[]{:S(2)}, u32[]{:S(2)}) async-start(bf16[64,32,576]{2,0,1:T(8,128)(2,1)} %copy.56), calls=%async_computation | async-start | bytes 5242880 | tf_op jit(solution)/shard_map/all_to_all | solution.py:101
  25.5 173.5 %all-gather.7.cloned.1.call-start = ((), (), s32[]{:S(2)}) async-start(), calls=%async_computation.2 | async-start | bytes 3899392 | tf_op jit(solution)/shard_map/all_gather | solution.py:93
  26.2 344.6 %all-reduce.2.cloned.1.call-start = ((), (), s32[]{:S(2)}) async-start(), calls=%async_computation.3 | async-start | bytes 3670016 | tf_op jit(solution)/shard_map/psum | solution.py:127
  117.4 17.5 %copy-start.4 = (pred[1024,2048]{0,1:T(8,128)(4,1)S(1)}, pred[1024,2048]{0,1:T(8,128)(4,1)}, u32[]{:S(2)}) copy-start(pred[1024,2048]{0,1:T(8,128)(4,1)} %iota_compare_fusion) | copy-start | bytes 6291460
  129.2 5.7 copy-start.2
  199.0 5.7 copy-start.5
  199.0 5.7 copy-start.6
  204.6 5.8 copy-start.8
  204.6 5.9 copy-start.10
  204.6 241.0 %copy-start.9 = (f32[7168]{0:T(1024)S(1)}, f32[7168]{0:T(1024)}, u32[]{:S(2)}) copy-start(f32[7168]{0:T(1024)} %param.20) | copy-start | bytes 86020
  208.7 237.0 %all-gather.9.cloned.1.call-start = ((), (), s32[]{:S(2)}) async-start(), calls=%async_computation.4 | async-start | bytes 3899392 | tf_op jit(solution)/shard_map/all_gather | solution.py:94
  209.2 308.7 %all-gather.11.cloned.1.call-start = ((), (), s32[]{:S(2)}) async-start(), calls=%async_computation.5 | async-start | bytes 3899392 | tf_op jit(solution)/shard_map/all_gather | solution.py:95
  209.8 380.3 %all-gather.13.cloned.1.call-start = ((), (), s32[]{:S(2)}) async-start(), calls=%async_computation.6 | async-start | bytes 3899392 | tf_op jit(solution)/shard_map/all_gather | solution.py:96
  210.4 576.5 %reduce-scatter.2.cloned.1.call-start = ((), (), s32[]{:S(2)}) async-start(), calls=%async_computation.7 | async-start | bytes 15597568 | tf_op jit(solution)/shard_map/reduce_scatter | solution.py:144
  596.4 15.6 %copy-start.3 = (bf16[7168,256]{1,0:T(8,128)(2,1)S(1)}, bf16[7168,256]{1,0:T(8,128)(2,1)}, u32[]{:S(2)}) copy-start(bf16[7168,256]{1,0:T(8,128)(2,1)} %all-gather.7.cloned.1.call-done) | copy-start | bytes 11010052
  629.1 160.1 %copy-start.1 = (bf16[2,512,128]{2,1,0:T(8,128)(2,1)S(1)}, bf16[2,512,128]{2,1,0:T(8,128)(2,1)}, u32[]{:S(2)}) copy-start(bf16[2,512,128]{2,1,0:T(8,128)(2,1)} %param.18) | copy-start | bytes 786436
Sparse Core Ops, SparseCore 0:
  9.6 107.7 all-gather.14
  120.1 78.8 all-gather.6
  208.8 161.9 all-reduce.1
  373.7 71.9 all-gather.8
  448.6 69.2 all-gather.10
  520.9 69.2 all-gather.12
  629.2 157.6 reduce-scatter.1
where the time goes:
time: 802 us; the launch traced here: 796 us
  waiting for transfers between devices  666 us (83%)
  matrix products  74.7 us (9%)
  local copies, waits for them, and re-layouts  18.2 us (2%)
  between operations  13.7 us (2%)
  other arithmetic  13.6 us (2%)
  starting transfers between devices  9.54 us (1%)
    psum x1, waiting for transfers between devices, body(): lax.psum(partial_rows.astype(jnp.bfloat16), 'ctx').astype(jnp.float32)  160 us
    reduce_scatter x1, waiting for transfers between devices, body(): lax.psum_scatter((head_term + jnp.einsum('sr,sd->rd', picker_wide, expert...  158 us
    all_gather x1, waiting for transfers between devices, body(): lax.all_gather(expert_gate, 'fsdp', axis=0, tiled=True)  73.4 us
    all_gather x1, waiting for transfers between devices, body(): lax.all_gather(expert_down, 'fsdp', axis=0, tiled=True)  72.2 us
    all_gather x1, waiting for transfers between devices, body(): lax.all_gather(expert_up, 'fsdp', axis=0, tiled=True)  69.1 us
    all_to_all x1, waiting for transfers between devices, body(): lax.all_to_all(query_local, 'ctx', split_axis=1, concat_axis=0, tiled=True)  55.2 us
    all_gather x1, waiting for transfers between devices, body(): lax.all_gather(out_proj, 'fsdp', axis=0, tiled=True)  48.4 us
    all_gather x1, waiting for transfers between devices, attend(): key_piece = lax.all_gather(key_local, 'ctx', axis=1, tiled=True)[0]  27.9 us
  transfers between devices with their start and end apart: 8, of which 8 were waited for; matrix products, arithmetic and copies ran while one was open for 6% of the time, Pallas kernels for 0%

commit v1 on v0

v1 whole, which is shorter than its diff:
```python
import functools

import jax
import jax.numpy as jnp
from jax import lax
from jax.experimental import pallas as pl
from jax.experimental.pallas import tpu as pltpu
from jax.sharding import PartitionSpec as P

MESH = pl.DeviceIdType.MESH
F32 = jnp.float32
BF16 = jnp.bfloat16

CAP = 4
SCALE_LOG2 = 192.0 ** (-0.5) * 1.4426950408889634
EPSILON = 1e-06
NEGATIVE = -1e30
N_SEND = 128
N_RECV = 128


def dot_nt(a, b):
    return lax.dot_general(a, b, (((1,), (1,)), ((), ())), preferred_element_type=F32)


def dot_nn(a, b):
    return jnp.dot(a, b, preferred_element_type=F32)


class Links:
    def __init__(self, send, recv):
        self.send, self.recv = send, recv
        self.n_send = self.n_recv = 0
        self.open = []

    def new_recv(self, count=1):
        base = self.n_recv
        self.n_recv += count
        assert self.n_recv <= N_RECV
        return base

    def start(self, src, dst, recv_index, device):
        copy = pltpu.make_async_remote_copy(
            src_ref=src,
            dst_ref=dst,
            send_sem=self.send.at[self.n_send],
            recv_sem=self.recv.at[recv_index],
            device_id=device,
            device_id_type=MESH,
        )
        self.n_send += 1
        assert self.n_send <= N_SEND
        copy.start()
        self.open.append(copy)

    def arrived(self, dst, recv_index, device):
        pltpu.make_async_remote_copy(
            src_ref=dst,
            dst_ref=dst,
            send_sem=self.send.at[0],
            recv_sem=self.recv.at[recv_index],
            device_id=device,
            device_id_type=MESH,
        ).wait_recv()

    def finish(self):
        for copy in self.open:
            copy.wait_send()


class Ring:
    def __init__(self, links, at, device, chunk, half):
        self.links, self.at, self.device = links, at, device
        self.chunk, self.half = chunk, half
        self.base = links.new_recv(4)
        self.up, self.down, self.far = (lax.rem(at + i, 4) for i in (1, 3, 2))

    def start(self):
        own = self.chunk(self.at)
        self.links.start(own, own, self.base, self.device(self.up))
        self.links.start(own, own, self.base + 1, self.device(self.down))

    def forward(self):
        self.links.arrived(self.chunk(self.down), self.base, self.device(self.down))
        part = self.half(self.down, 0)
        self.links.start(part, part, self.base + 2, self.device(self.up))
        self.links.arrived(self.chunk(self.up), self.base + 1, self.device(self.up))
        part = self.half(self.up, 1)
        self.links.start(part, part, self.base + 3, self.device(self.down))

    def finish(self):
        self.links.arrived(self.half(self.far, 0), self.base + 2, self.device(self.down))
        self.links.arrived(self.half(self.far, 1), self.base + 3, self.device(self.up))


def kernel(
    lens, hid, q, span, cache, gain, route_row, weight_row,
    vu_in, wo_in, wg_in, wu_in, wd_in,
    out,
    kb, kc, qs, vbuf, wbuf, wo, att, ho, hb,
    part, rsa, rsb, zsend, zrecv, mixed, normed,
    sb, sblk, yb, dp, dpa, dpb, zb, zr,
    send_sems, recv_sems, local_sems,
):
    c, f = lax.axis_index("ctx"), lax.axis_index("fsdp")
    z, y = c // 4, lax.rem(c, 4)
    zh, x, k = f // 8, lax.rem(f // 2, 4), lax.rem(f, 2)
    zm = lax.rem(z, 2)
    expert = z // 2
    links = Links(send_sems, recv_sems)

    def at_z(z2):
        return {"ctx": z2 * 4 + y, "fsdp": f}

    def at_y(y2):
        return {"ctx": z * 4 + y2, "fsdp": f}

    def at_x(x2):
        return {"ctx": c, "fsdp": zh * 8 + x2 * 2 + k}

    def at_zh(z2, zh2):
        return {"ctx": z2 * 4 + y, "fsdp": zh2 * 8 + x * 2 + k}

    other_core = {"ctx": c, "fsdp": zh * 8 + x * 2 + (1 - k)}
    far_half = at_zh(z, 1 - zh)
    pair = at_z(z + 1 - 2 * zm)
    zs = [lax.rem(z + i, 4) for i in range(4)]
    ys = [lax.rem(y + i, 4) for i in range(4)]
    xs = [lax.rem(x + i, 4) for i in range(4)]

    local = []

    def place(src, dst):
        copy = pltpu.make_async_copy(src, dst, local_sems.at[len(local)])
        copy.start()
        local.append(copy)

    place(cache, kb.at[0, c])
    place(span, kb.at[1, c])
    place(vu_in.at[k, pl.ds(pl.multiple_of(x * 128, 128), 128)], vbuf.at[k, x, z, y])
    for i, ref in enumerate((wg_in, wu_in, wd_in)):
        place(ref, wbuf.at[i, zh, x, k])

    barrier = pltpu.get_barrier_semaphore()
    peers = [at_y(ys[i]) for i in (1, 2, 3)] + [at_x(xs[i]) for i in (1, 2, 3)] + [other_core]
    peers += [at_zh(zs[i], zh) for i in (1, 2, 3)] + [at_zh(zs[i], 1 - zh) for i in range(4)]
    for peer in peers:
        pl.semaphore_signal(barrier, inc=1, device_id=peer, device_id_type=MESH)
    pl.semaphore_wait(barrier, len(peers))
    for copy in local:
        copy.wait()

    keys_z = links.new_recv(3)
    for i in (1, 2, 3):
        links.start(kb.at[:, c], kb.at[:, c], keys_z + i - 1, at_z(zs[i]))
    keys_y = []
    for i in range(4):
        zi = zs[i]
        keys_y.append(
            Ring(
                links, y, at_y,
                lambda o, zi=zi: kb.at[:, zi * 4 + o],
                lambda o, j, zi=zi: kb.at[j, zi * 4 + o],
            )
        )
    keys_y[0].start()
    vu_z = links.new_recv(3)
    for i in (1, 2, 3):
        own = vbuf.at[k, x, z, y]
        links.start(own, own, vu_z + i - 1, at_z(zs[i]))
    vu_y = Ring(
        links, y, at_y,
        lambda o: vbuf.at[k, x, :, o],
        lambda o, j: vbuf.at[k, x, pl.ds(2 * j, 2), o],
    )
    vu_x = Ring(
        links, x, at_x,
        lambda o: vbuf.at[k, o],
        lambda o, j: vbuf.at[k, o, pl.ds(2 * j, 2)],
    )
    gud_x = [
        Ring(
            links, x, at_x,
            lambda o, h=h: wbuf.at[:, h, o, k],
            lambda o, j, h=h: wbuf.at[:, h, o, k, pl.ds(224 * j, 224)],
        )
        for h in (zh, 1 - zh)
    ]
    gud_x[0].start()
    out_x = Ring(
        links, x, at_x,
        lambda o: wo.at[:, o, k],
        lambda o, j: wo.at[pl.ds(2 * j, 2), o, k],
    )

    def relayout(index, carry):
        zq, yq = index // 4, lax.rem(index, 4)
        cols = q[:, pl.ds(pl.multiple_of(index * 1152, 128), 1152)]
        qs[yq, zq, 0] = cols[:, :576]
        qs[yq, zq, 1] = cols[:, 576:]
        return carry

    lax.fori_loop(0, 8, relayout, 0)

    for i in (1, 2, 3):
        links.arrived(kb.at[:, zs[4 - i] * 4 + y], keys_z + i - 1, at_z(zs[4 - i]))
        keys_y[4 - i].start()

    out_z = links.new_recv(4)
    out_sends = []
    for a in range(2):
        for b in range(2):
            z2 = zh + 2 * a
            own = (z2 == z) & (zh == b)
            sem = links.n_send
            links.n_send += 1

            def remote(sem=sem, z2=z2, b=b):
                return pltpu.make_async_remote_copy(
                    src_ref=wo_in,
                    dst_ref=wo.at[z, x, k],
                    send_sem=send_sems.at[sem],
                    recv_sem=recv_sems.at[out_z + z],
                    device_id=at_zh(z2, b),
                    device_id_type=MESH,
                )

            @pl.when(own)
            def _():
                pltpu.make_async_copy(wo_in, wo.at[z, x, k], recv_sems.at[out_z + z]).start()

            @pl.when(jnp.logical_not(own))
            def _():
                remote().start()

            out_sends.append((own, remote))

    for i in (1, 2, 3):
        links.arrived(vbuf.at[k, x, zs[4 - i], y], vu_z + i - 1, at_z(zs[4 - i]))
    vu_y.start()

    lax.fori_loop(8, 16, relayout, 0)

    order = (0, 3, 2, 1)
    for i in order:
        keys_y[i].forward()
    vu_y.forward()
    for i in order:
        keys_y[i].finish()
    vu_y.finish()
    vu_x.start()
    gud_x[0].forward()

    slot = lax.broadcasted_iota(jnp.int32, (512, 128), 0)
    lane = lax.broadcasted_iota(jnp.int32, (512, 128), 1)
    packed = None
    first = 0
    for b in range(0, 16, 2):
        len0, len1 = lens[0, b], lens[0, b + 1]
        left = (lane < len0) & (slot == lane + first)
        right = (lane >= 64) & (lane < 64 + len1) & (slot == lane - 64 + (first + len0))
        pick = jnp.where(left & (lane < 64) | right, 1.0, 0.0).astype(BF16)
        term = dot_nn(pick, kb[0, pl.ds(b, 2)].reshape(128, 576))
        packed = term if packed is None else packed + term
        first = first + len0 + len1
    kc[...] = packed.astype(BF16)

    def attend(group):
        def step(half, carry):
            rows = qs[group, pl.ds(2 * half, 2)].reshape(256, 576)
            s1 = dot_nt(rows, kc[...])
            s2 = dot_nt(rows, kb[1].reshape(1024, 576))
            token = lax.rem(lax.broadcasted_iota(jnp.int32, (256, 1024), 0), 64)
            key = lax.broadcasted_iota(jnp.int32, (256, 1024), 1)
            s2 = jnp.where(key <= token + c * 64, s2, NEGATIVE)
            top = jnp.maximum(
                jnp.max(s1, axis=1, keepdims=True), jnp.max(s2, axis=1, keepdims=True)
            )
            p1 = jnp.exp2((s1 - top) * SCALE_LOG2)
            p2 = jnp.exp2((s2 - top) * SCALE_LOG2)
            total = jnp.sum(p1, axis=1, keepdims=True) + jnp.sum(p2, axis=1, keepdims=True)
            acc = dot_nn(p1.astype(BF16), kc[:, :512])
            acc = acc + dot_nn(p2.astype(BF16), kb[1, :, :, :512].reshape(1024, 512))
            att[group, pl.ds(2 * half, 2)] = (acc / total).astype(BF16).reshape(2, 2, 64, 512)
            return carry

        lax.fori_loop(0, 2, step, 0)

    attend(ys[1])
    for i in range(4):
        links.arrived(wo.at[i, x, k], out_z + i, at_z(zs[1]))
    out_x.start()
    out_core = links.new_recv(4)
    links.start(wo.at[:, x, k], wo.at[:, x, k], out_core, other_core)
    gud_z = links.new_recv(1)
    mine = wbuf.at[:, zh, x, k]
    links.start(mine, mine, gud_z, far_half)

    attend(ys[2])
    vu_x.forward()
    attend(ys[3])
    vu_x.finish()
    vu_core = links.new_recv(1)
    links.start(vbuf.at[k], vbuf.at[k], vu_core, other_core)
    attend(ys[0])
    out_x.forward()
    for i in (1, 3):
        links.start(wo.at[:, xs[i], k], wo.at[:, xs[i], k], out_core + i, other_core)
    gud_x[0].finish()
    gud_core = links.new_recv(2)
    ready = wbuf.at[:, zh, :, k]
    links.start(ready, ready, gud_core, other_core)
    links.arrived(vbuf.at[1 - k], vu_core, other_core)

    ho_y = links.new_recv(4)
    for i in (1, 2, 3, 0):
        group = ys[i]
        for zq in range(4):
            pieces = []
            for j in range(2):
                value = jnp.concatenate([vbuf[j, r, zq, group] for r in range(4)], axis=0)
                pieces.append(dot_nn(att[group, zq, j], value).astype(BF16))
            ho[i, :, zq * 256 : (zq + 1) * 256] = jnp.concatenate(pieces, axis=1)
        if i:
            links.start(ho.at[i], hb.at[y, zm], ho_y + i, at_y(group))
        else:
            hb[y, zm] = ho[0]
    ho_z = links.new_recv(4)
    links.start(ho.at[0], hb.at[y, zm], ho_z, pair)
    for i in (1, 2, 3):
        source = ys[4 - i]
        links.arrived(hb.at[source, zm], ho_y + i, at_y(source))
        links.start(hb.at[source, zm], hb.at[source, zm], ho_z + i, pair)
    out_x.finish()
    links.start(wo.at[:, xs[2], k], wo.at[:, xs[2], k], out_core + 2, other_core)
    for i in range(4):
        source = ys[(4 - i) % 4]
        links.arrived(hb.at[source, 1 - zm], ho_z + i, pair)

    rs_a, rs_b, rs_z = links.new_recv(8), links.new_recv(8), links.new_recv(4)
    tiles = (0, 1, 3, 2)

    def project(n):
        i = tiles[n]
        links.arrived(wo.at[:, xs[i], 1 - k], out_core + i, other_core)
        acc = None
        for zq in range(4):
            term = dot_nt(
                hb[:, :, :, zq * 256 : (zq + 1) * 256].reshape(512, 256),
                wo[zq, xs[i]].reshape(896, 256),
            )
            acc = term if acc is None else acc + term
        part[n] = acc.astype(BF16).reshape(4, 2, 64, 896)
        links.start(part.at[n, ys[2], 0], rsa.at[n, 0], rs_a + 2 * n, at_y(ys[1]))
        links.start(part.at[n, ys[2], 1], rsa.at[n, 1], rs_a + 2 * n + 1, at_y(ys[3]))

    def pass_on(n):
        links.arrived(rsa.at[n, 0], rs_a + 2 * n, at_y(ys[3]))
        part[n, ys[1], 0] = (part[n, ys[1], 0].astype(F32) + rsa[n, 0].astype(F32)).astype(BF16)
        links.start(part.at[n, ys[1]], rsb.at[n, 0], rs_b + 2 * n, at_y(ys[1]))
        links.arrived(rsa.at[n, 1], rs_a + 2 * n + 1, at_y(ys[1]))
        part[n, ys[3], 1] = (part[n, ys[3], 1].astype(F32) + rsa[n, 1].astype(F32)).astype(BF16)
        links.start(part.at[n, ys[3]], rsb.at[n, 1], rs_b + 2 * n + 1, at_y(ys[3]))

    def columns(half, n):
        return pl.ds(pl.multiple_of(half * 3584 + xs[tiles[n]] * 896, 128), 896)

    def collect(n):
        links.arrived(rsb.at[n, 0], rs_b + 2 * n, at_y(ys[3]))
        links.arrived(rsb.at[n, 1], rs_b + 2 * n + 1, at_y(ys[1]))

        def total(member):
            return (
                part[n, y, member].astype(F32)
                + rsb[n, 0, member].astype(F32)
                + rsb[n, 1, member].astype(F32)
            )

        zsend[n] = total(1 - zm).astype(BF16)
        links.start(zsend.at[n], zrecv.at[n], rs_z + n, pair)
        cols = columns(zm, n)
        mixed[:, cols] = hid[:, cols].astype(F32) + total(zm)

    project(0)
    project(1)
    pass_on(0)
    links.arrived(wbuf.at[:, 1 - zh, x, k], gud_z, far_half)
    gud_x[1].start()
    project(2)
    pass_on(1)
    collect(0)
    project(3)
    pass_on(2)
    collect(1)
    pass_on(3)
    collect(2)
    collect(3)
    for n in range(4):
        links.arrived(zrecv.at[n], rs_z + n, pair)
        cols = columns(1 - zm, n)
        mixed[:, cols] = hid[:, cols].astype(F32) + zrecv[n].astype(F32)
    gud_x[1].forward()

    square = None
    for r in range(8):
        block = mixed[:, r * 896 : (r + 1) * 896]
        term = jnp.sum(block * block, axis=1, keepdims=True)
        square = term if square is None else square + term
    inverse = lax.rsqrt(square * (1.0 / 7168.0) + EPSILON)
    for r in range(8):
        cols = slice(r * 896, (r + 1) * 896)
        normed[:, cols] = (mixed[:, cols] * inverse * gain[:, cols]).astype(BF16)

    earlier = lax.broadcasted_iota(jnp.int32, (64, 64), 1) < lax.broadcasted_iota(
        jnp.int32, (64, 64), 0
    )
    earlier = jnp.where(earlier, 1.0, 0.0).astype(BF16)
    lane16 = lax.broadcasted_iota(jnp.int32, (64, 128), 1)
    chosen, gates = [], []
    for e in range(2):
        match = route_row[...] == e
        hit = jnp.sum(jnp.where(match, 1.0, 0.0), axis=1, keepdims=True)
        gates.append(jnp.sum(jnp.where(match, weight_row[...], 0.0), axis=1, keepdims=True))
        wide = jnp.broadcast_to(hit, (64, 128))
        within = dot_nn(earlier, wide.astype(BF16))
        for p in range(4):
            pick = (wide > 0.5) & (lane16 // 4 == p) & (within.astype(jnp.int32) == lax.rem(lane16, 4))
            chosen.append(jnp.where(pick, 1.0, 0.0))
    for e in range(2):
        block = None
        for p in range(4):
            pick = jnp.transpose(chosen[4 * e + p])[:16].astype(BF16)
            term = dot_nn(pick, normed[:, p * 1792 : (p + 1) * 1792])
            block = term if block is None else block + term
        sb[e] = block.astype(BF16)
    sl_z = links.new_recv(3)
    for i in (1, 2, 3):
        links.start(sb.at[zs[i] // 2], sblk.at[z], sl_z + i - 1, at_z(zs[i]))
    sblk[z] = sb[expert]
    for i in (1, 2, 3):
        links.arrived(sblk.at[zs[4 - i]], sl_z + i - 1, at_z(zs[4 - i]))
    stacked = sblk[...].reshape(64, 1792)
    row = lax.broadcasted_iota(jnp.int32, (16, 64), 0)
    col = lax.broadcasted_iota(jnp.int32, (16, 64), 1)
    same = (row // 4 == col // 16) & (lax.rem(row, 4) == lax.rem(col, 4))
    for p in range(4):
        pick = jnp.where(same & (lax.rem(col, 16) // 4 == p), 1.0, 0.0).astype(BF16)
        yb[y, p] = dot_nn(pick, stacked).astype(BF16)
    sl_y = Ring(
        links, y, at_y,
        lambda o: yb.at[o],
        lambda o, j: yb.at[o, pl.ds(2 * j, 2)],
    )
    sl_y.start()
    gud_x[1].finish()
    ready = wbuf.at[:, 1 - zh, :, k]
    links.start(ready, ready, gud_core + 1, other_core)
    sl_y.forward()
    links.arrived(wbuf.at[:, zh, :, 1 - k], gud_core, other_core)
    sl_y.finish()
    links.arrived(wbuf.at[:, 1 - zh, :, 1 - k], gud_core + 1, other_core)

    gate_acc = up_acc = None
    for p in range(4):
        rows = yb[:, p].reshape(64, 1792)
        span_x = pl.ds(2 * (p % 2), 2)
        g_term = dot_nn(rows, wbuf[0, p // 2, span_x].reshape(1792, 256))
        u_term = dot_nn(rows, wbuf[1, p // 2, span_x].reshape(1792, 256))
        gate_acc = g_term if gate_acc is None else gate_acc + g_term
        up_acc = u_term if up_acc is None else up_acc + u_term
    act = (gate_acc / (1.0 + jnp.exp(-gate_acc)) * up_acc).astype(BF16)
    for p in range(4):
        down = dot_nt(act, wbuf[2, p // 2, pl.ds(2 * (p % 2), 2)].reshape(1792, 256))
        dp[:, p] = down.astype(BF16).reshape(4, 16, 1792)

    d_a, d_b = links.new_recv(2), links.new_recv(2)
    links.start(dp.at[ys[2], pl.ds(0, 2)], dpa.at[0], d_a, at_y(ys[1]))
    links.start(dp.at[ys[2], pl.ds(2, 2)], dpa.at[1], d_a + 1, at_y(ys[3]))
    links.arrived(dpa.at[0], d_a, at_y(ys[3]))
    head = pl.ds(0, 2)
    dp[ys[1], head] = (dp[ys[1], head].astype(F32) + dpa[0].astype(F32)).astype(BF16)
    links.start(dp.at[ys[1]], dpb.at[0], d_b, at_y(ys[1]))
    links.arrived(dpa.at[1], d_a + 1, at_y(ys[1]))
    tail = pl.ds(2, 2)
    dp[ys[3], tail] = (dp[ys[3], tail].astype(F32) + dpa[1].astype(F32)).astype(BF16)
    links.start(dp.at[ys[3]], dpb.at[1], d_b + 1, at_y(ys[3]))
    links.arrived(dpb.at[0], d_b, at_y(ys[3]))
    links.arrived(dpb.at[1], d_b + 1, at_y(ys[1]))
    row = lax.broadcasted_iota(jnp.int32, (64, 16), 0)
    col = lax.broadcasted_iota(jnp.int32, (64, 16), 1)
    same = (row // 16 == col // 4) & (lax.rem(row, 4) == lax.rem(col, 4))
    blocks = None
    for p in range(4):
        total = dp[y, p].astype(F32) + dpb[0, p].astype(F32) + dpb[1, p].astype(F32)
        pick = jnp.where(same & (lax.rem(row, 16) // 4 == p), 1.0, 0.0).astype(BF16)
        term = dot_nn(pick, total.astype(BF16))
        blocks = term if blocks is None else blocks + term
    zb[...] = blocks.astype(BF16).reshape(4, 16, 1792)
    d_z = links.new_recv(3)
    for i in (1, 2, 3):
        links.start(zb.at[zs[i]], zr.at[z], d_z + i - 1, at_z(zs[i]))
    zr[z] = zb[z]
    for i in (1, 2, 3):
        links.arrived(zr.at[zs[4 - i]], d_z + i - 1, at_z(zs[4 - i]))

    for p in range(4):
        cols = slice(p * 1792, (p + 1) * 1792)
        value = mixed[:, cols]
        for e in range(2):
            pick = chosen[4 * e + p][:, :16].astype(BF16)
            rows = dot_nn(pick, zr[2 * e]) + dot_nn(pick, zr[2 * e + 1])
            value = value + gates[e] * rows
        out[:, cols] = value.astype(BF16)

    links.finish()
    for own, remote in out_sends:

        @pl.when(jnp.logical_not(own))
        def _():
            remote().wait_send()


def body(
    hidden_in, queries, span_latent, cache_latent, cache_len, value_up, out_proj, norm_gain,
    expert_gate, expert_up, expert_down, routes, route_weights,
):
    c = lax.axis_index("ctx")
    route_row = lax.dynamic_slice_in_dim(routes[0], c * 64, 64, 0)
    weight_row = lax.dynamic_slice_in_dim(route_weights[0], c * 64, 64, 0)
    vmem = pl.BlockSpec(memory_space=pltpu.VMEM)
    hbm = pl.BlockSpec(memory_space=pl.ANY)
    smem = pl.BlockSpec(memory_space=pltpu.SMEM)
    result = pl.pallas_call(
        kernel,
        out_shape=jax.ShapeDtypeStruct((64, 7168), BF16),
        in_specs=[smem, vmem, vmem, vmem, vmem, vmem, vmem, vmem, hbm, hbm, hbm, hbm, hbm],
        out_specs=vmem,
        scratch_shapes=[
            pltpu.VMEM((2, 16, 64, 576), BF16),
            pltpu.VMEM((512, 576), BF16),
            pltpu.VMEM((4, 4, 2, 64, 576), BF16),
            pltpu.VMEM((2, 4, 4, 4, 128, 128), BF16),
            pltpu.VMEM((3, 2, 4, 2, 448, 256), BF16),
            pltpu.VMEM((4, 4, 2, 448, 256), BF16),
            pltpu.VMEM((4, 4, 2, 64, 512), BF16),
            pltpu.VMEM((4, 64, 1024), BF16),
            pltpu.VMEM((4, 2, 64, 1024), BF16),
            pltpu.VMEM((4, 4, 2, 64, 896), BF16),
            pltpu.VMEM((4, 2, 64, 896), BF16),
            pltpu.VMEM((4, 2, 2, 64, 896), BF16),
            pltpu.VMEM((4, 64, 896), BF16),
            pltpu.VMEM((4, 64, 896), BF16),
            pltpu.VMEM((64, 7168), F32),
            pltpu.VMEM((64, 7168), BF16),
            pltpu.VMEM((2, 16, 1792), BF16),
            pltpu.VMEM((4, 16, 1792), BF16),
            pltpu.VMEM((4, 4, 16, 1792), BF16),
            pltpu.VMEM((4, 4, 16, 1792), BF16),
            pltpu.VMEM((2, 2, 16, 1792), BF16),
            pltpu.VMEM((2, 4, 16, 1792), BF16),
            pltpu.VMEM((4, 16, 1792), BF16),
            pltpu.VMEM((4, 16, 1792), BF16),
            pltpu.SemaphoreType.DMA((N_SEND,)),
            pltpu.SemaphoreType.DMA((N_RECV,)),
            pltpu.SemaphoreType.DMA((8,)),
        ],
        compiler_params=pltpu.CompilerParams(
            collective_id=0, has_side_effects=True, vmem_limit_bytes=60 * 1024 * 1024
        ),
        name="layer",
    )(
        cache_len, hidden_in[0], queries[0], span_latent[0], cache_latent[0],
        norm_gain[None], route_row, weight_row,
        value_up, out_proj, expert_gate, expert_up, expert_down,
    )
    return result[None]


def solution(mesh):
    in_specs = (
        P("fsdp", "ctx", None),
        P("fsdp", "ctx", None),
        P("fsdp", "ctx", None),
        P("fsdp", "ctx", None),
        P("fsdp", None),
        P("ctx", None, None),
        P("fsdp", "ctx"),
        P(),
        P("fsdp", "ctx"),
        P("fsdp", "ctx"),
        P("fsdp", "ctx"),
        P("fsdp", None, None),
        P("fsdp", None, None),
    )
    out_specs = P("fsdp", "ctx", None)
    return jax.shard_map(body, mesh=mesh, in_specs=in_specs, out_specs=out_specs, check_vma=False)
```

time: 802 us -> 215 us (0.27)
  waiting for transfers between devices: 666 us -> 0 us
  Pallas kernels: 0 us -> 206 us
  matrix products: 74.7 us -> 0 us
  between operations: 13.7 us -> 0.01 us
  other arithmetic: 13.6 us -> 0 us
  local copies, waits for them, and re-layouts: 18.2 us -> 5.14 us
  starting transfers between devices: 9.54 us -> 0 us
    all_gather x5 -> x0, waiting for transfers between devices: 291 us -> none  [the longest x1 73.4 us: body(): lax.all_gather(expert_gate, 'fsdp', axis=0, tiled=True)]
    pallas_call x0 -> x1, Pallas kernels: none -> 206 us  [body(): pl.pallas_call(kernel, out_shape=jax.ShapeDtypeStruct((64, 7168), BF16),...]
    psum x1 -> x0, waiting for transfers between devices: 160 us -> none  [body(): lax.psum(partial_rows.astype(jnp.bfloat16), 'ctx').astype(jnp.float32)]
    reduce_scatter x1 -> x0, waiting for transfers between devices: 158 us -> none  [body(): lax.psum_scatter((head_term + jnp.einsum('sr,sd->rd', picker_wide, expert...]
    dot_general x8 -> x0, matrix products: 74.7 us -> none  [the longest x1 17.1 us: body(): jnp.einsum('rj,dj->rd', head_out, proj_full, preferred_element_type=jnp.f...]
    all_to_all x1 -> x0, waiting for transfers between devices: 55.2 us -> none  [body(): lax.all_to_all(query_local, 'ctx', split_axis=1, concat_axis=0, tiled=True)]
    all_to_all x1 -> x0, starting transfers between devices: 9.12 us -> none  [body(): lax.all_to_all(query_local, 'ctx', split_axis=1, concat_axis=0, tiled=True)]
  transfers between devices with their start and end apart: 8 -> 0, of which waited for: 8 -> 0; matrix products, arithmetic and copies ran while one was open for 6% -> 0% of each run, Pallas kernels for 0% -> 0%
where the time goes in v1:
time: 215 us; the launch traced here: 212 us
  Pallas kernels  206 us (96%)
  local copies, waits for them, and re-layouts  5.14 us (2%)
    pallas_call x1, Pallas kernels, body(): pl.pallas_call(kernel, out_shape=jax.ShapeDtypeStruct((64, 7168), BF16),...  206 us

profile of v1, /device:TPU:10, one launch (start us, length us, event | category | flops | bytes accessed | tf_op | source)
XLA Modules:
  0.0 211.7 jit_solution(6767379492241990769)
XLA Ops:
  0.0 0.0 copy-start
  0.0 0.8 copy-done
  0.8 0.1 constant_dynamic-slice_fusion.1
  0.8 0.8 constant_dynamic-slice_fusion
  1.6 0.7 copy.15
  2.3 0.7 copy.14
  3.0 206.5 %layer.1 = bf16[64,7168]{1,0:T(8,128)(2,1)} custom-call(s32[1,16]{1,0:T(1,128)} %lens.1, bf16[64,7168]{1,0:T(8,128)(2,1)} %bitcast.10, bf16[64,18432]{1,0:T(8,128)(2,1)} %bitcast.9, bf16[64,576]{1,0:T(8,128)(2,1)} %bitcast.13, bf16[64,576]{1,0:T(8,128)(2,1)} %bitcast.14, f32[1,7168]{1,0:T(1,128)} %bitcast.15, s32[64,8]{1,0:T(8,128)} %bitcast.12, ...), custom_call_target="tpu_custom_call" | custom-call | tf_op jit(solution)/shard_map/layer/pallas_call | solution.py:533
  209.5 2.2 %copy.17 = bf16[1,64,7168]{2,1,0:T(8,128)(2,1)} copy(bf16[1,64,7168]{2,1,0:T(8,128)(2,1)} %bitcast.8) | data formatting | bytes 1835008
Async XLA Ops:
  0.0 0.8 copy-start

commit v2 on v1

--- a/solution.py
+++ b/solution.py
@@ -94,19 +94,20 @@
 
 
 def kernel(
-    lens, hid, q, span, cache, gain, route_row, weight_row,
+    lens, hid_in, q_in, span, cache, gain, routes_in, weights_in,
     vu_in, wo_in, wg_in, wu_in, wd_in,
     out,
     kb, kc, qs, vbuf, wbuf, wo, att, ho, hb,
-    part, rsa, rsb, zsend, zrecv, mixed, normed,
-    sb, sblk, yb, dp, dpa, dpb, zb, zr,
+    part, rsa, rsb, zsend, zrecv, mixed, sel, hs, sp, sq, sx, sy, nrm,
+    sb, sblk, yb, dp, dpa, dpb, zb, zr, hid, q, routes, weights,
     send_sems, recv_sems, local_sems,
 ):
     c, f = lax.axis_index("ctx"), lax.axis_index("fsdp")
     z, y = c // 4, lax.rem(c, 4)
     zh, x, k = f // 8, lax.rem(f // 2, 4), lax.rem(f, 2)
     zm = lax.rem(z, 2)
-    expert = z // 2
+    place_z = zh * 4 + z
+    expert = 1 - z // 2
     links = Links(send_sems, recv_sems)
 
     def at_z(z2):
@@ -122,8 +123,14 @@
         return {"ctx": z2 * 4 + y, "fsdp": zh2 * 8 + x * 2 + k}
 
     other_core = {"ctx": c, "fsdp": zh * 8 + x * 2 + (1 - k)}
-    far_half = at_zh(z, 1 - zh)
-    pair = at_z(z + 1 - 2 * zm)
+    up_two, down_two = lax.rem(place_z + 2, 8), lax.rem(place_z + 6, 8)
+    twos = [at_zh(lax.rem(p, 4), p // 4) for p in (up_two, down_two)]
+    partner = z + 1 - 2 * zm
+    pair = at_z(partner)
+
+    def at_pair(y2):
+        return {"ctx": partner * 4 + y2, "fsdp": f}
+
     zs = [lax.rem(z + i, 4) for i in range(4)]
     ys = [lax.rem(y + i, 4) for i in range(4)]
     xs = [lax.rem(x + i, 4) for i in range(4)]
@@ -138,21 +145,57 @@
     place(cache, kb.at[0, c])
     place(span, kb.at[1, c])
     place(vu_in.at[k, pl.ds(pl.multiple_of(x * 128, 128), 128)], vbuf.at[k, x, z, y])
-    for i, ref in enumerate((wg_in, wu_in, wd_in)):
-        place(ref, wbuf.at[i, zh, x, k])
+    place(q_in, q)
+    place(hid_in, hid)
+    place(routes_in, routes)
+    place(weights_in, weights)
 
     barrier = pltpu.get_barrier_semaphore()
     peers = [at_y(ys[i]) for i in (1, 2, 3)] + [at_x(xs[i]) for i in (1, 2, 3)] + [other_core]
     peers += [at_zh(zs[i], zh) for i in (1, 2, 3)] + [at_zh(zs[i], 1 - zh) for i in range(4)]
+    peers += [at_pair(ys[i]) for i in (1, 2, 3)]
     for peer in peers:
         pl.semaphore_signal(barrier, inc=1, device_id=peer, device_id_type=MESH)
     pl.semaphore_wait(barrier, len(peers))
-    for copy in local:
+    for copy in local[:3]:
         copy.wait()
 
+    vu_z = links.new_recv(3)
+    for i in (1, 2, 3):
+        own = vbuf.at[k, x, z, y]
+        links.start(own, own, vu_z + i - 1, at_z(zs[i]))
     keys_z = links.new_recv(3)
     for i in (1, 2, 3):
         links.start(kb.at[:, c], kb.at[:, c], keys_z + i - 1, at_z(zs[i]))
+    out_z = links.new_recv(4)
+    out_sends = []
+    for a in range(2):
+        for b in range(2):
+            z2 = zh + 2 * a
+            own = (z2 == z) & (zh == b)
+            sem = links.n_send
+            links.n_send += 1
+
+            def remote(sem=sem, z2=z2, b=b):
+                return pltpu.make_async_remote_copy(
+                    src_ref=wo_in,
+                    dst_ref=wo.at[z, x, k],
+                    send_sem=send_sems.at[sem],
+                    recv_sem=recv_sems.at[out_z + z],
+                    device_id=at_zh(z2, b),
+                    device_id_type=MESH,
+                )
+
+            @pl.when(own)
+            def _():
+                pltpu.make_async_copy(wo_in, wo.at[z, x, k], recv_sems.at[out_z + z]).start()
+
+            @pl.when(jnp.logical_not(own))
+            def _():
+                remote().start()
+
+            out_sends.append((own, remote))
+
     keys_y = []
     for i in range(4):
         zi = zs[i]
@@ -164,10 +207,6 @@
             )
         )
     keys_y[0].start()
-    vu_z = links.new_recv(3)
-    for i in (1, 2, 3):
-        own = vbuf.at[k, x, z, y]
-        links.start(own, own, vu_z + i - 1, at_z(zs[i]))
     vu_y = Ring(
         links, y, at_y,
         lambda o: vbuf.at[k, x, :, o],
@@ -178,20 +217,30 @@
         lambda o: vbuf.at[k, o],
         lambda o, j: vbuf.at[k, o, pl.ds(2 * j, 2)],
     )
-    gud_x = [
-        Ring(
-            links, x, at_x,
-            lambda o, h=h: wbuf.at[:, h, o, k],
-            lambda o, j, h=h: wbuf.at[:, h, o, k, pl.ds(224 * j, 224)],
-        )
-        for h in (zh, 1 - zh)
-    ]
-    gud_x[0].start()
+    gu_x = Ring(
+        links, x, at_x,
+        lambda o: wbuf.at[pl.ds(0, 2), :, o, k],
+        lambda o, j: wbuf.at[pl.ds(0, 2), j, o, k],
+    )
+    down_x = Ring(
+        links, x, at_x,
+        lambda o: wbuf.at[2, :, o, k],
+        lambda o, j: wbuf.at[2, j, o, k],
+    )
     out_x = Ring(
         links, x, at_x,
         lambda o: wo.at[:, o, k],
         lambda o, j: wo.at[pl.ds(2 * j, 2), o, k],
     )
+    expert_z = links.new_recv(6)
+
+    def send_expert(w, ref):
+        for p in twos:
+            links.start(ref, wbuf.at[w, zh, x, k], expert_z + 2 * w + zh, p)
+
+    def got_expert(w):
+        for h in range(2):
+            links.arrived(wbuf.at[w, h, x, k], expert_z + 2 * w + h, twos[0])
 
     def relayout(index, carry):
         zq, yq = index // 4, lax.rem(index, 4)
@@ -200,56 +249,94 @@
         qs[yq, zq, 1] = cols[:, 576:]
         return carry
 
-    lax.fori_loop(0, 8, relayout, 0)
-
-    for i in (1, 2, 3):
+    for i in (1, 2, 3):
+        links.arrived(vbuf.at[k, x, zs[4 - i], y], vu_z + i - 1, at_z(zs[4 - i]))
+    vu_y.start()
+    local[3].wait()
+    lax.fori_loop(0, 16, relayout, 0)
+    vu_y.forward()
+
+    for copy in local[4:]:
+        copy.wait()
+    near = pl.ds(pl.multiple_of((c // 2) * 128, 128), 128)
+
+    def own_tokens(ref):
+        both = ref[:, near]
+        return jnp.where(lax.rem(c, 2) == 1, both[:, 64:], both[:, :64])
+
+    own_routes, own_weights = own_tokens(routes), own_tokens(weights)
+    earlier = lax.broadcasted_iota(jnp.int32, (64, 64), 0) < lax.broadcasted_iota(
+        jnp.int32, (64, 64), 1
+    )
+    earlier = jnp.where(earlier, 1.0, 0.0).astype(BF16)
+    slot_row = lax.broadcasted_iota(jnp.int32, (128, 64), 0)
+    chosen, gates, mine = [], [], []
+    for e in range(2):
+        match = own_routes == e
+        hit = jnp.sum(jnp.where(match, 1.0, 0.0), axis=0, keepdims=True)
+        weight = jnp.sum(jnp.where(match, own_weights, 0.0), axis=0, keepdims=True)
+        within = dot_nn(jnp.broadcast_to(hit, (16, 64)).astype(BF16), earlier)[:1]
+        named = (hit > 0.5) & (within.astype(jnp.int32) == lax.rem(slot_row, 4))
+        mine.append((hit, within))
+        for p in range(4):
+            chosen.append(jnp.where(named & (slot_row // 4 == p), 1.0, 0.0))
+        gates.append(
+            jnp.sum(jnp.where(named & (slot_row < 16), weight, 0.0)[:16], axis=1, keepdims=True)
+        )
+
+    pair_routes = routes[:, pl.ds(pl.multiple_of((z // 2) * 512, 128), 512)]
+    row = lax.broadcasted_iota(jnp.int32, (128, 128), 0)
+    col = lax.broadcasted_iota(jnp.int32, (128, 128), 1)
+    earlier = jnp.where((row < col) & (row // 64 == col // 64), 1.0, 0.0).astype(BF16)
+    hits, places = [], []
+    for e in range(2):
+        hit = jnp.sum(jnp.where(pair_routes == e, 1.0, 0.0), axis=0, keepdims=True)
+        wide = jnp.broadcast_to(hit, (16, 512)).astype(BF16)
+        counts = [dot_nn(wide[:, i * 128 : (i + 1) * 128], earlier)[:1] for i in range(4)]
+        hits.append(hit)
+        places.append(jnp.concatenate(counts, axis=1))
+    row = lax.broadcasted_iota(jnp.int32, (64, 512), 0)
+    col = lax.broadcasted_iota(jnp.int32, (64, 512), 1)
+    first = lax.rem(row // 4, 2) == 0
+    hit = jnp.where(first, hits[0], hits[1])
+    place_of = jnp.where(first, places[0], places[1]).astype(jnp.int32)
+    here = (row // 16 == lax.rem(col // 64, 4)) & (lax.rem(row // 8, 2) == col // 256)
+    pick = here & (hit > 0.5) & (place_of == lax.rem(row, 4))
+    sel[...] = jnp.where(pick, 1.0, 0.0).astype(BF16)
+    row = lax.broadcasted_iota(jnp.int32, (16, 64), 0)
+    first = lax.rem(row // 4, 2) == 0
+    hit = jnp.where(first, mine[0][0], mine[1][0])
+    place_of = jnp.where(first, mine[0][1], mine[1][1]).astype(jnp.int32)
+    pick = (row // 8 == zm) & (hit > 0.5) & (place_of == lax.rem(row, 4))
+    own_slots = jnp.where(pick, 1.0, 0.0).astype(BF16)
+
+
+    def key_block(i):
         links.arrived(kb.at[:, zs[4 - i] * 4 + y], keys_z + i - 1, at_z(zs[4 - i]))
         keys_y[4 - i].start()
 
-    out_z = links.new_recv(4)
-    out_sends = []
-    for a in range(2):
-        for b in range(2):
-            z2 = zh + 2 * a
-            own = (z2 == z) & (zh == b)
-            sem = links.n_send
-            links.n_send += 1
-
-            def remote(sem=sem, z2=z2, b=b):
-                return pltpu.make_async_remote_copy(
-                    src_ref=wo_in,
-                    dst_ref=wo.at[z, x, k],
-                    send_sem=send_sems.at[sem],
-                    recv_sem=recv_sems.at[out_z + z],
-                    device_id=at_zh(z2, b),
-                    device_id_type=MESH,
-                )
-
-            @pl.when(own)
-            def _():
-                pltpu.make_async_copy(wo_in, wo.at[z, x, k], recv_sems.at[out_z + z]).start()
-
-            @pl.when(jnp.logical_not(own))
-            def _():
-                remote().start()
-
-            out_sends.append((own, remote))
-
-    for i in (1, 2, 3):
-        links.arrived(vbuf.at[k, x, zs[4 - i], y], vu_z + i - 1, at_z(zs[4 - i]))
-    vu_y.start()
-
-    lax.fori_loop(8, 16, relayout, 0)
-
-    order = (0, 3, 2, 1)
-    for i in order:
-        keys_y[i].forward()
-    vu_y.forward()
-    for i in order:
-        keys_y[i].finish()
+    key_block(1)
+    keys_y[0].forward()
     vu_y.finish()
     vu_x.start()
-    gud_x[0].forward()
+    key_block(2)
+    keys_y[3].forward()
+    key_block(3)
+
+    keys_y[2].forward()
+    keys_y[1].forward()
+    vu_x.forward()
+    vu_core = links.new_recv(1)
+    out_core = links.new_recv(4)
+    gu_core, down_core = links.new_recv(1), links.new_recv(1)
+    for i in range(4):
+        links.arrived(wo.at[i, x, k], out_z + i, at_z(zs[1]))
+    out_x.start()
+    links.start(wo.at[:, x, k], wo.at[:, x, k], out_core, other_core)
+    send_expert(0, wg_in)
+    send_expert(1, wu_in)
+    for i in (0, 3, 2, 1):
+        keys_y[i].finish()
 
     slot = lax.broadcasted_iota(jnp.int32, (512, 128), 0)
     lane = lax.broadcasted_iota(jnp.int32, (512, 128), 1)
@@ -286,34 +373,9 @@
 
         lax.fori_loop(0, 2, step, 0)
 
-    attend(ys[1])
-    for i in range(4):
-        links.arrived(wo.at[i, x, k], out_z + i, at_z(zs[1]))
-    out_x.start()
-    out_core = links.new_recv(4)
-    links.start(wo.at[:, x, k], wo.at[:, x, k], out_core, other_core)
-    gud_z = links.new_recv(1)
-    mine = wbuf.at[:, zh, x, k]
-    links.start(mine, mine, gud_z, far_half)
-
-    attend(ys[2])
-    vu_x.forward()
-    attend(ys[3])
-    vu_x.finish()
-    vu_core = links.new_recv(1)
-    links.start(vbuf.at[k], vbuf.at[k], vu_core, other_core)
-    attend(ys[0])
-    out_x.forward()
-    for i in (1, 3):
-        links.start(wo.at[:, xs[i], k], wo.at[:, xs[i], k], out_core + i, other_core)
-    gud_x[0].finish()
-    gud_core = links.new_recv(2)
-    ready = wbuf.at[:, zh, :, k]
-    links.start(ready, ready, gud_core, other_core)
-    links.arrived(vbuf.at[1 - k], vu_core, other_core)
-
-    ho_y = links.new_recv(4)
-    for i in (1, 2, 3, 0):
+    ho_y, ho_z = links.new_recv(4), links.new_recv(4)
+
+    def head_outputs(i):
         group = ys[i]
         for zq in range(4):
             pieces = []
@@ -321,28 +383,34 @@
                 value = jnp.concatenate([vbuf[j, r, zq, group] for r in range(4)], axis=0)
                 pieces.append(dot_nn(att[group, zq, j], value).astype(BF16))
             ho[i, :, zq * 256 : (zq + 1) * 256] = jnp.concatenate(pieces, axis=1)
+        links.start(ho.at[i], hb.at[zm, y], ho_z + i, at_pair(group))
         if i:
-            links.start(ho.at[i], hb.at[y, zm], ho_y + i, at_y(group))
+            links.start(ho.at[i], hb.at[zm, y], ho_y + i, at_y(group))
         else:
-            hb[y, zm] = ho[0]
-    ho_z = links.new_recv(4)
-    links.start(ho.at[0], hb.at[y, zm], ho_z, pair)
-    for i in (1, 2, 3):
-        source = ys[4 - i]
-        links.arrived(hb.at[source, zm], ho_y + i, at_y(source))
-        links.start(hb.at[source, zm], hb.at[source, zm], ho_z + i, pair)
-    out_x.finish()
-    links.start(wo.at[:, xs[2], k], wo.at[:, xs[2], k], out_core + 2, other_core)
-    for i in range(4):
-        source = ys[(4 - i) % 4]
-        links.arrived(hb.at[source, 1 - zm], ho_z + i, pair)
+            hb[zm, y] = ho[0]
+
+    vu_x.finish()
+    links.start(vbuf.at[k], vbuf.at[k], vu_core, other_core)
+    attend(ys[2])
+    attend(ys[1])
+    links.arrived(vbuf.at[1 - k], vu_core, other_core)
+    head_outputs(2)
+    head_outputs(1)
+    attend(ys[3])
+    head_outputs(3)
+    attend(ys[0])
+    head_outputs(0)
+    out_x.forward()
+    for i in (1, 3):
+        links.start(wo.at[:, xs[i], k], wo.at[:, xs[i], k], out_core + i, other_core)
+    got_expert(0)
+    got_expert(1)
 
     rs_a, rs_b, rs_z = links.new_recv(8), links.new_recv(8), links.new_recv(4)
     tiles = (0, 1, 3, 2)
 
     def project(n):
         i = tiles[n]
-        links.arrived(wo.at[:, xs[i], 1 - k], out_core + i, other_core)
         acc = None
         for zq in range(4):
             term = dot_nt(
@@ -350,17 +418,17 @@
                 wo[zq, xs[i]].reshape(896, 256),
             )
             acc = term if acc is None else acc + term
-        part[n] = acc.astype(BF16).reshape(4, 2, 64, 896)
-        links.start(part.at[n, ys[2], 0], rsa.at[n, 0], rs_a + 2 * n, at_y(ys[1]))
-        links.start(part.at[n, ys[2], 1], rsa.at[n, 1], rs_a + 2 * n + 1, at_y(ys[3]))
+        part[n] = acc.astype(BF16).reshape(2, 4, 64, 896)
+        links.start(part.at[n, 0, ys[2]], rsa.at[n, 0], rs_a + 2 * n, at_y(ys[1]))
+        links.start(part.at[n, 1, ys[2]], rsa.at[n, 1], rs_a + 2 * n + 1, at_y(ys[3]))
 
     def pass_on(n):
         links.arrived(rsa.at[n, 0], rs_a + 2 * n, at_y(ys[3]))
-        part[n, ys[1], 0] = (part[n, ys[1], 0].astype(F32) + rsa[n, 0].astype(F32)).astype(BF16)
-        links.start(part.at[n, ys[1]], rsb.at[n, 0], rs_b + 2 * n, at_y(ys[1]))
+        part[n, 0, ys[1]] = (part[n, 0, ys[1]].astype(F32) + rsa[n, 0].astype(F32)).astype(BF16)
+        links.start(part.at[n, :, ys[1]], rsb.at[n, 0], rs_b + 2 * n, at_y(ys[1]))
         links.arrived(rsa.at[n, 1], rs_a + 2 * n + 1, at_y(ys[1]))
-        part[n, ys[3], 1] = (part[n, ys[3], 1].astype(F32) + rsa[n, 1].astype(F32)).astype(BF16)
-        links.start(part.at[n, ys[3]], rsb.at[n, 1], rs_b + 2 * n + 1, at_y(ys[3]))
+        part[n, 1, ys[3]] = (part[n, 1, ys[3]].astype(F32) + rsa[n, 1].astype(F32)).astype(BF16)
+        links.start(part.at[n, :, ys[3]], rsb.at[n, 1], rs_b + 2 * n + 1, at_y(ys[3]))
 
     def columns(half, n):
         return pl.ds(pl.multiple_of(half * 3584 + xs[tiles[n]] * 896, 128), 896)
@@ -371,7 +439,7 @@
 
         def total(member):
             return (
-                part[n, y, member].astype(F32)
+                part[n, member, y].astype(F32)
                 + rsb[n, 0, member].astype(F32)
                 + rsb[n, 1, member].astype(F32)
             )
@@ -381,62 +449,74 @@
         cols = columns(zm, n)
         mixed[:, cols] = hid[:, cols].astype(F32) + total(zm)
 
+    def slot_tile(n):
+        i = tiles[n]
+        links.arrived(wo.at[:, xs[i], 1 - k], out_core + i, other_core)
+        acc = None
+        for zq in range(4):
+            term = dot_nt(hs[:, zq * 256 : (zq + 1) * 256], wo[zq, xs[i]].reshape(896, 256))
+            acc = term if acc is None else acc + term
+        sp[:, xs[i]] = acc.astype(BF16).reshape(4, 16, 896)
+
+    for i in (2, 1, 3, 0):
+        source = ys[(4 - i) % 4]
+        if i:
+            links.arrived(hb.at[zm, source], ho_y + i, at_y(source))
+        links.arrived(hb.at[1 - zm, source], ho_z + i, at_pair(source))
+    hs[...] = dot_nn(sel[...], hb[...].reshape(512, 1024)).astype(BF16)
+    slot_tile(0)
     project(0)
+    slot_tile(1)
+    slot_tile(2)
+    out_x.finish()
+    links.start(wo.at[:, xs[2], k], wo.at[:, xs[2], k], out_core + 2, other_core)
+    gu_x.start()
+    send_expert(2, wd_in)
+    slot_tile(3)
+    slot_y, slot_z = links.new_recv(3), links.new_recv(1)
+    for i in (1, 2, 3):
+        links.start(sp.at[ys[i]], sq.at[i - 1], slot_y + i - 1, at_y(ys[i]))
     project(1)
+    for i in (1, 2, 3):
+        links.arrived(sq.at[i - 1], slot_y + i - 1, at_y(ys[4 - i]))
+    half = sp[y].astype(F32) + sq[0].astype(F32) + sq[1].astype(F32) + sq[2].astype(F32)
+    sx[...] = half.astype(BF16)
+    links.start(sx, sy, slot_z, pair)
+    nrm[zm] = half
     pass_on(0)
-    links.arrived(wbuf.at[:, 1 - zh, x, k], gud_z, far_half)
-    gud_x[1].start()
     project(2)
+    links.arrived(sy, slot_z, pair)
+    nrm[1 - zm] = sy[...].astype(F32)
+    square = None
+    for r in range(8):
+        cols = slice(r * 896, (r + 1) * 896)
+        block = nrm[r // 4, r % 4] + dot_nn(own_slots, hid[:, cols])
+        nrm[r // 4, r % 4] = block
+        term = jnp.sum(block * block, axis=1, keepdims=True)
+        square = term if square is None else square + term
+    inverse = lax.rsqrt(square * (1.0 / 7168.0) + EPSILON)
+    row = lax.broadcasted_iota(jnp.int32, (16, 16), 0)
+    col = lax.broadcasted_iota(jnp.int32, (16, 16), 1)
+    blocks = [None, None]
+    for p in range(4):
+        pieces = []
+        for r in (2 * p, 2 * p + 1):
+            cols = slice(r * 896, (r + 1) * 896)
+            pieces.append((nrm[r // 4, r % 4] * inverse * gain[:, cols]).astype(BF16))
+        rows = jnp.concatenate(pieces, axis=1)
+        for e in range(2):
+            pick = (row // 4 == p) & (col == zm * 8 + e * 4 + lax.rem(row, 4))
+            term = dot_nn(jnp.where(pick, 1.0, 0.0).astype(BF16), rows)
+            blocks[e] = term if blocks[e] is None else blocks[e] + term
+    for e in range(2):
+        sb[e] = blocks[e].astype(BF16)
+    sl_z = links.new_recv(3)
+    for i in (1, 2, 3):
+        links.start(sb.at[1 - zs[i] // 2], sblk.at[z], sl_z + i - 1, at_z(zs[i]))
+    sblk[z] = sb[expert]
     pass_on(1)
     collect(0)
     project(3)
-    pass_on(2)
-    collect(1)
-    pass_on(3)
-    collect(2)
-    collect(3)
-    for n in range(4):
-        links.arrived(zrecv.at[n], rs_z + n, pair)
-        cols = columns(1 - zm, n)
-        mixed[:, cols] = hid[:, cols].astype(F32) + zrecv[n].astype(F32)
-    gud_x[1].forward()
-
-    square = None
-    for r in range(8):
-        block = mixed[:, r * 896 : (r + 1) * 896]
-        term = jnp.sum(block * block, axis=1, keepdims=True)
-        square = term if square is None else square + term
-    inverse = lax.rsqrt(square * (1.0 / 7168.0) + EPSILON)
-    for r in range(8):
-        cols = slice(r * 896, (r + 1) * 896)
-        normed[:, cols] = (mixed[:, cols] * inverse * gain[:, cols]).astype(BF16)
-
-    earlier = lax.broadcasted_iota(jnp.int32, (64, 64), 1) < lax.broadcasted_iota(
-        jnp.int32, (64, 64), 0
-    )
-    earlier = jnp.where(earlier, 1.0, 0.0).astype(BF16)
-    lane16 = lax.broadcasted_iota(jnp.int32, (64, 128), 1)
-    chosen, gates = [], []
-    for e in range(2):
-        match = route_row[...] == e
-        hit = jnp.sum(jnp.where(match, 1.0, 0.0), axis=1, keepdims=True)
-        gates.append(jnp.sum(jnp.where(match, weight_row[...], 0.0), axis=1, keepdims=True))
-        wide = jnp.broadcast_to(hit, (64, 128))
-        within = dot_nn(earlier, wide.astype(BF16))
-        for p in range(4):
-            pick = (wide > 0.5) & (lane16 // 4 == p) & (within.astype(jnp.int32) == lax.rem(lane16, 4))
-            chosen.append(jnp.where(pick, 1.0, 0.0))
-    for e in range(2):
-        block = None
-        for p in range(4):
-            pick = jnp.transpose(chosen[4 * e + p])[:16].astype(BF16)
-            term = dot_nn(pick, normed[:, p * 1792 : (p + 1) * 1792])
-            block = term if block is None else block + term
-        sb[e] = block.astype(BF16)
-    sl_z = links.new_recv(3)
-    for i in (1, 2, 3):
-        links.start(sb.at[zs[i] // 2], sblk.at[z], sl_z + i - 1, at_z(zs[i]))
-    sblk[z] = sb[expert]
     for i in (1, 2, 3):
         links.arrived(sblk.at[zs[4 - i]], sl_z + i - 1, at_z(zs[4 - i]))
     stacked = sblk[...].reshape(64, 1792)
@@ -452,13 +532,19 @@
         lambda o, j: yb.at[o, pl.ds(2 * j, 2)],
     )
     sl_y.start()
-    gud_x[1].finish()
-    ready = wbuf.at[:, 1 - zh, :, k]
-    links.start(ready, ready, gud_core + 1, other_core)
+    gu_x.forward()
+    got_expert(2)
+    down_x.start()
+    pass_on(2)
     sl_y.forward()
-    links.arrived(wbuf.at[:, zh, :, 1 - k], gud_core, other_core)
+    collect(1)
+    pass_on(3)
+    gu_x.finish()
+    ready = wbuf.at[pl.ds(0, 2), :, :, k]
+    links.start(ready, ready, gu_core, other_core)
     sl_y.finish()
-    links.arrived(wbuf.at[:, 1 - zh, :, 1 - k], gud_core + 1, other_core)
+    down_x.forward()
+    links.arrived(wbuf.at[pl.ds(0, 2), :, :, 1 - k], gu_core, other_core)
 
     gate_acc = up_acc = None
     for p in range(4):
@@ -468,11 +554,16 @@
         u_term = dot_nn(rows, wbuf[1, p // 2, span_x].reshape(1792, 256))
         gate_acc = g_term if gate_acc is None else gate_acc + g_term
         up_acc = u_term if up_acc is None else up_acc + u_term
+    down_x.finish()
+    links.start(wbuf.at[2, :, :, k], wbuf.at[2, :, :, k], down_core, other_core)
     act = (gate_acc / (1.0 + jnp.exp(-gate_acc)) * up_acc).astype(BF16)
+    links.arrived(wbuf.at[2, :, :, 1 - k], down_core, other_core)
     for p in range(4):
         down = dot_nt(act, wbuf[2, p // 2, pl.ds(2 * (p % 2), 2)].reshape(1792, 256))
         dp[:, p] = down.astype(BF16).reshape(4, 16, 1792)
 
+    collect(2)
+    collect(3)
     d_a, d_b = links.new_recv(2), links.new_recv(2)
     links.start(dp.at[ys[2], pl.ds(0, 2)], dpa.at[0], d_a, at_y(ys[1]))
     links.start(dp.at[ys[2], pl.ds(2, 2)], dpa.at[1], d_a + 1, at_y(ys[3]))
@@ -500,16 +591,22 @@
     for i in (1, 2, 3):
         links.start(zb.at[zs[i]], zr.at[z], d_z + i - 1, at_z(zs[i]))
     zr[z] = zb[z]
+    for n in range(4):
+        links.arrived(zrecv.at[n], rs_z + n, pair)
+        cols = columns(1 - zm, n)
+        mixed[:, cols] = hid[:, cols].astype(F32) + zrecv[n].astype(F32)
     for i in (1, 2, 3):
         links.arrived(zr.at[zs[4 - i]], d_z + i - 1, at_z(zs[4 - i]))
 
+    for e in range(2):
+        rows = zr[2 - 2 * e].astype(F32) + zr[3 - 2 * e].astype(F32)
+        sblk[e] = (rows * gates[e]).astype(BF16)
     for p in range(4):
         cols = slice(p * 1792, (p + 1) * 1792)
         value = mixed[:, cols]
         for e in range(2):
-            pick = chosen[4 * e + p][:, :16].astype(BF16)
-            rows = dot_nn(pick, zr[2 * e]) + dot_nn(pick, zr[2 * e + 1])
-            value = value + gates[e] * rows
+            pick = jnp.transpose(chosen[4 * e + p])[:, :16].astype(BF16)
+            value = value + dot_nn(pick, sblk[e])
         out[:, cols] = value.astype(BF16)
 
     links.finish()
@@ -524,16 +621,13 @@
     hidden_in, queries, span_latent, cache_latent, cache_len, value_up, out_proj, norm_gain,
     expert_gate, expert_up, expert_down, routes, route_weights,
 ):
-    c = lax.axis_index("ctx")
-    route_row = lax.dynamic_slice_in_dim(routes[0], c * 64, 64, 0)
-    weight_row = lax.dynamic_slice_in_dim(route_weights[0], c * 64, 64, 0)
     vmem = pl.BlockSpec(memory_space=pltpu.VMEM)
     hbm = pl.BlockSpec(memory_space=pl.ANY)
     smem = pl.BlockSpec(memory_space=pltpu.SMEM)
     result = pl.pallas_call(
         kernel,
         out_shape=jax.ShapeDtypeStruct((64, 7168), BF16),
-        in_specs=[smem, vmem, vmem, vmem, vmem, vmem, vmem, vmem, hbm, hbm, hbm, hbm, hbm],
+        in_specs=[smem, hbm, hbm, hbm, hbm, vmem, hbm, hbm, hbm, hbm, hbm, hbm, hbm],
         out_specs=vmem,
         scratch_shapes=[
             pltpu.VMEM((2, 16, 64, 576), BF16),
@@ -544,14 +638,20 @@
             pltpu.VMEM((4, 4, 2, 448, 256), BF16),
             pltpu.VMEM((4, 4, 2, 64, 512), BF16),
             pltpu.VMEM((4, 64, 1024), BF16),
-            pltpu.VMEM((4, 2, 64, 1024), BF16),
-            pltpu.VMEM((4, 4, 2, 64, 896), BF16),
+            pltpu.VMEM((2, 4, 64, 1024), BF16),
+            pltpu.VMEM((4, 2, 4, 64, 896), BF16),
             pltpu.VMEM((4, 2, 64, 896), BF16),
             pltpu.VMEM((4, 2, 2, 64, 896), BF16),
             pltpu.VMEM((4, 64, 896), BF16),
             pltpu.VMEM((4, 64, 896), BF16),
             pltpu.VMEM((64, 7168), F32),
-            pltpu.VMEM((64, 7168), BF16),
+            pltpu.VMEM((64, 512), BF16),
+            pltpu.VMEM((64, 1024), BF16),
+            pltpu.VMEM((4, 4, 16, 896), BF16),
+            pltpu.VMEM((3, 4, 16, 896), BF16),
+            pltpu.VMEM((4, 16, 896), BF16),
+            pltpu.VMEM((4, 16, 896), BF16),
+            pltpu.VMEM((2, 4, 16, 896), F32),
             pltpu.VMEM((2, 16, 1792), BF16),
             pltpu.VMEM((4, 16, 1792), BF16),
             pltpu.VMEM((4, 4, 16, 1792), BF16),
@@ -560,6 +660,10 @@
             pltpu.VMEM((2, 4, 16, 1792), BF16),
             pltpu.VMEM((4, 16, 1792), BF16),
             pltpu.VMEM((4, 16, 1792), BF16),
+            pltpu.VMEM((64, 7168), BF16),
+            pltpu.VMEM((64, 18432), BF16),
+            pltpu.VMEM((8, 1024), jnp.int32),
+            pltpu.VMEM((8, 1024), F32),
             pltpu.SemaphoreType.DMA((N_SEND,)),
             pltpu.SemaphoreType.DMA((N_RECV,)),
             pltpu.SemaphoreType.DMA((8,)),
@@ -570,7 +674,7 @@
         name="layer",
     )(
         cache_len, hidden_in[0], queries[0], span_latent[0], cache_latent[0],
-        norm_gain[None], route_row, weight_row,
+        norm_gain[None], routes[0].T, route_weights[0].T,
         value_up, out_proj, expert_gate, expert_up, expert_down,
     )
     return result[None]

time: 215 us -> 165 us (0.77)
  Pallas kernels: 206 us -> 161 us
  local copies, waits for them, and re-layouts: 5.14 us -> 2.16 us
    pallas_call x1, Pallas kernels: 206 us -> 161 us  [body(): pl.pallas_call(kernel, out_shape=jax.ShapeDtypeStruct((64, 7168), BF16),...]
    dynamic_slice x4 -> x0, local copies, waits for them, and re-layouts: 2.23 us -> none  [the longest x2 1.46 us: body(): weight_row = lax.dynamic_slice_in_dim(route_weights[0], c * 64, 64, 0)]
where the time goes in v2:
time: 165 us; the launch traced here: 163 us
  Pallas kernels  161 us (98%)
  local copies, waits for them, and re-layouts  2.16 us (1%)
    pallas_call x1, Pallas kernels, body(): pl.pallas_call(kernel, out_shape=jax.ShapeDtypeStruct((64, 7168), BF16),...  161 us

profile of v2, /device:TPU:10, one launch (start us, length us, event | category | flops | bytes accessed | tf_op | source)
XLA Modules:
  0.0 163.1 jit_solution(12761991332662781263)
XLA Ops:
  0.0 160.9 %layer.1 = bf16[64,7168]{1,0:T(8,128)(2,1)} custom-call(s32[1,16]{1,0:T(1,128)} %lens.1, bf16[64,7168]{1,0:T(8,128)(2,1)} %bitcast.14, bf16[64,18432]{1,0:T(8,128)(2,1)} %bitcast.13, bf16[64,576]{1,0:T(8,128)(2,1)} %bitcast.15, bf16[64,576]{1,0:T(8,128)(2,1)} %bitcast.16, f32[1,7168]{1,0:T(1,128)} %bitcast.19, s32[8,1024]{1,0:T(8,128)} %bitcast.17, ...), custom_call_target="tpu_custom_call" | custom-call | tf_op jit(solution)/shard_map/layer/pallas_call | solution.py:627
  160.9 2.2 %copy.15 = bf16[1,64,7168]{2,1,0:T(8,128)(2,1)} copy(bf16[1,64,7168]{2,1,0:T(8,128)(2,1)} %bitcast.12) | data formatting | bytes 1835008

commit v3 on v2

--- a/solution.py
+++ b/solution.py
@@ -516,7 +516,9 @@
     sblk[z] = sb[expert]
     pass_on(1)
     collect(0)
-    project(3)
+    gu_x.forward()
+    got_expert(2)
+    down_x.start()
     for i in (1, 2, 3):
         links.arrived(sblk.at[zs[4 - i]], sl_z + i - 1, at_z(zs[4 - i]))
     stacked = sblk[...].reshape(64, 1792)
@@ -532,18 +534,14 @@
         lambda o, j: yb.at[o, pl.ds(2 * j, 2)],
     )
     sl_y.start()
-    gu_x.forward()
-    got_expert(2)
-    down_x.start()
     pass_on(2)
     sl_y.forward()
-    collect(1)
-    pass_on(3)
     gu_x.finish()
     ready = wbuf.at[pl.ds(0, 2), :, :, k]
     links.start(ready, ready, gu_core, other_core)
     sl_y.finish()
     down_x.forward()
+    project(3)
     links.arrived(wbuf.at[pl.ds(0, 2), :, :, 1 - k], gu_core, other_core)
 
     gate_acc = up_acc = None
@@ -557,16 +555,17 @@
     down_x.finish()
     links.start(wbuf.at[2, :, :, k], wbuf.at[2, :, :, k], down_core, other_core)
     act = (gate_acc / (1.0 + jnp.exp(-gate_acc)) * up_acc).astype(BF16)
+    collect(1)
+    pass_on(3)
     links.arrived(wbuf.at[2, :, :, 1 - k], down_core, other_core)
     for p in range(4):
         down = dot_nt(act, wbuf[2, p // 2, pl.ds(2 * (p % 2), 2)].reshape(1792, 256))
         dp[:, p] = down.astype(BF16).reshape(4, 16, 1792)
 
-    collect(2)
-    collect(3)
     d_a, d_b = links.new_recv(2), links.new_recv(2)
     links.start(dp.at[ys[2], pl.ds(0, 2)], dpa.at[0], d_a, at_y(ys[1]))
     links.start(dp.at[ys[2], pl.ds(2, 2)], dpa.at[1], d_a + 1, at_y(ys[3]))
+    collect(2)
     links.arrived(dpa.at[0], d_a, at_y(ys[3]))
     head = pl.ds(0, 2)
     dp[ys[1], head] = (dp[ys[1], head].astype(F32) + dpa[0].astype(F32)).astype(BF16)
@@ -575,6 +574,7 @@
     tail = pl.ds(2, 2)
     dp[ys[3], tail] = (dp[ys[3], tail].astype(F32) + dpa[1].astype(F32)).astype(BF16)
     links.start(dp.at[ys[3]], dpb.at[1], d_b + 1, at_y(ys[3]))
+    collect(3)
     links.arrived(dpb.at[0], d_b, at_y(ys[3]))
     links.arrived(dpb.at[1], d_b + 1, at_y(ys[1]))
     row = lax.broadcasted_iota(jnp.int32, (64, 16), 0)

time: 165 us -> 164 us (level); the launches traced: 163 us -> 164 us
  no operation moved by 1% of the time
where the time goes in v3:
time: 164 us
  Pallas kernels  162 us (99%)
  local copies, waits for them, and re-layouts  2.16 us (1%)
    pallas_call x1, Pallas kernels, body(): pl.pallas_call(kernel, out_shape=jax.ShapeDtypeStruct((64, 7168), BF16),...  162 us

profile of v3, /device:TPU:10, one launch (start us, length us, event | category | flops | bytes accessed | tf_op | source)
XLA Modules:
  0.0 164.1 jit_solution(14069056678825689324)
XLA Ops:
  0.0 161.9 %layer.1 = bf16[64,7168]{1,0:T(8,128)(2,1)} custom-call(s32[1,16]{1,0:T(1,128)} %lens.1, bf16[64,7168]{1,0:T(8,128)(2,1)} %bitcast.14, bf16[64,18432]{1,0:T(8,128)(2,1)} %bitcast.13, bf16[64,576]{1,0:T(8,128)(2,1)} %bitcast.15, bf16[64,576]{1,0:T(8,128)(2,1)} %bitcast.16, f32[1,7168]{1,0:T(1,128)} %bitcast.19, s32[8,1024]{1,0:T(8,128)} %bitcast.17, ...), custom_call_target="tpu_custom_call" | custom-call | tf_op jit(solution)/shard_map/layer/pallas_call | solution.py:627
  161.9 2.2 %copy.15 = bf16[1,64,7168]{2,1,0:T(8,128)(2,1)} copy(bf16[1,64,7168]{2,1,0:T(8,128)(2,1)} %bitcast.12) | data formatting | bytes 1835008

commit v4 on v3

--- a/solution.py
+++ b/solution.py
@@ -334,7 +334,6 @@
     out_x.start()
     links.start(wo.at[:, x, k], wo.at[:, x, k], out_core, other_core)
     send_expert(0, wg_in)
-    send_expert(1, wu_in)
     for i in (0, 3, 2, 1):
         keys_y[i].finish()
 
@@ -400,11 +399,10 @@
     head_outputs(3)
     attend(ys[0])
     head_outputs(0)
+    send_expert(1, wu_in)
     out_x.forward()
     for i in (1, 3):
         links.start(wo.at[:, xs[i], k], wo.at[:, xs[i], k], out_core + i, other_core)
-    got_expert(0)
-    got_expert(1)
 
     rs_a, rs_b, rs_z = links.new_recv(8), links.new_recv(8), links.new_recv(4)
     tiles = (0, 1, 3, 2)
@@ -470,6 +468,8 @@
     slot_tile(2)
     out_x.finish()
     links.start(wo.at[:, xs[2], k], wo.at[:, xs[2], k], out_core + 2, other_core)
+    got_expert(0)
+    got_expert(1)
     gu_x.start()
     send_expert(2, wd_in)
     slot_tile(3)

time: 164 us -> 163 us (level)
  no operation moved by 1% of the time
where the time goes in v4:
time: 163 us
  Pallas kernels  161 us (99%)
  local copies, waits for them, and re-layouts  2.16 us (1%)
    pallas_call x1, Pallas kernels, body(): pl.pallas_call(kernel, out_shape=jax.ShapeDtypeStruct((64, 7168), BF16),...  161 us

profile of v4, /device:TPU:10, one launch (start us, length us, event | category | flops | bytes accessed | tf_op | source)
XLA Modules:
  0.0 162.7 jit_solution(1582046417319924300)
XLA Ops:
  0.0 160.5 %layer.1 = bf16[64,7168]{1,0:T(8,128)(2,1)} custom-call(s32[1,16]{1,0:T(1,128)} %lens.1, bf16[64,7168]{1,0:T(8,128)(2,1)} %bitcast.14, bf16[64,18432]{1,0:T(8,128)(2,1)} %bitcast.13, bf16[64,576]{1,0:T(8,128)(2,1)} %bitcast.15, bf16[64,576]{1,0:T(8,128)(2,1)} %bitcast.16, f32[1,7168]{1,0:T(1,128)} %bitcast.19, s32[8,1024]{1,0:T(8,128)} %bitcast.17, ...), custom_call_target="tpu_custom_call" | custom-call | tf_op jit(solution)/shard_map/layer/pallas_call | solution.py:627
  160.5 2.2 %copy.15 = bf16[1,64,7168]{2,1,0:T(8,128)(2,1)} copy(bf16[1,64,7168]{2,1,0:T(8,128)(2,1)} %bitcast.12) | data formatting | bytes 1835008
